TPU v7x, 32 devices: a whole 2x2x4 slice. The times are simulated.
32 devices in a mesh: req: 8 (over z, x), mlp: 4 (over y, core).
Axes of the slice: x: 2, y: 2, z: 4, core: 2. Of those that a mesh axis runs over, the one named last changes fastest.
Arguments:
- tokens: bfloat16 [4096, 4096], P('req'), may hold values from -16 to 16
- grid_sides: int32 [16, 2], P('req'), may hold values from 10 to 14, as said below
- offsets: int32 [16], P('req'), may hold values from 0 to 201, as said below
- merge_rows: int32 [1024, 4], P('req'), may hold values from 0 to 401, as said below
- routes: int32 [1024, 1], replicated, may hold values from 0 to 7; in each aligned block of 128 rows (0 to 127, 128 to 255, ...) at most 16 rows name the same one
- norm_gain: float32 [2, 4096], replicated, may hold values from 0.5 to 1.5
- norm_bias: float32 [2, 4096], replicated, may hold values from -1.5 to 1.5
- layer_scale: float32 [2, 4096], replicated, may hold values from 0.2 to 1
- qkv_weight: bfloat16 [4096, 6144], P('req', 'mlp'), may hold values from -2.34375 to 2.34375
- out_weight: bfloat16 [2048, 4096], P('mlp', 'req'), may hold values from -0.125 to 0.125
- gate_up: bfloat16 [2, 4096, 4096], P(None, 'req', 'mlp'), may hold values from -0.09375 to 0.09375
- down_weight: bfloat16 [4096, 4096], P('mlp', 'req'), may hold values from -0.09375 to 0.09375
- merge_gain: float32 [4, 4096], P(None, 'mlp'), may hold values from 0.5 to 1.5
- merge_bias: float32 [4, 4096], P(None, 'mlp'), may hold values from -1.5 to 1.5
- merge_weight: bfloat16 [4, 4096, 2048], P(None, 'mlp', 'req'), may hold values from -0.1875 to 0.1875
Outputs:
- embeds: bfloat16 [1024, 2048], P('req', 'mlp')
- token_norms: float32 [1024], P('req')
- max_logits: float32 [16, 16], P('req', 'mlp')
Inputs may be any that keep to these rules, and one draw needn't show every extreme that they name: `grid_sides`: sides are even; the first 2 of all 16 images are 14 x 14 and the last image is 10 x 10. `offsets`: the images of a group are packed in order from in-group row 0: image g * 2 + j starts at the sum of 5 + h w over images g * 2 to g * 2 + j - 1. `merge_rows`: for slot k of group g, image i = g * 2 + k div 64 of grid h x w at offset o and m = k mod 64: if m < (h / 2)(w / 2), the entries are o + 5 + (2 a + e) w + 2 b + f for (e, f) = (0, 0), (0, 1), (1, 0), (1, 1), with a = m div (w / 2), b = m mod (w / 2); otherwise all four are 0. `routes`: among the 128 slots of one group, no value appears more than 16 times.
All inputs are finite; a program needn't handle non-finite values.
Results may differ from a plain program's by a relative error of at most 0.017.
Values may be sent and summed in bfloat16 or wider, within the bound.
A program may use at most 128 MiB of HBM per device.

v0:
```python
import math
import jax
import jax.numpy as jnp
from jax import lax
from jax.sharding import PartitionSpec as P

HEAD = 128
OUT = 2048
MSLOT = 64
CAP = 16
EPS = 1e-06


def layer_norm(values, scale_vec, shift_vec):
    center = jnp.mean(values, axis=-1, keepdims=True)
    offset_vals = values - center
    spread = jnp.mean(offset_vals * offset_vals, axis=-1, keepdims=True)
    return offset_vals * lax.rsqrt(spread + EPS) * scale_vec + shift_vec


def row_layout(grid_part, starts, row_count, head_size):
    position = jnp.arange(row_count, dtype=jnp.int32)
    lengths = 5 + grid_part[:, 0] * grid_part[:, 1]
    inside = (
        (position[:, None] >= starts[None, :]) & (position[:, None] < (starts + lengths)[None, :])
    ).astype(jnp.int32)
    present = jnp.sum(inside, axis=1)
    numbers = jnp.arange(grid_part.shape[0], dtype=jnp.int32)
    image_id = jnp.sum(inside * numbers[None, :], axis=1) + present - 1
    local_row = position - jnp.sum(inside * starts[None, :], axis=1)
    height = jnp.sum(inside * grid_part[None, :, 0], axis=1) + 1 - present
    breadth = jnp.sum(inside * grid_part[None, :, 1], axis=1) + 1 - present
    is_patch = (local_row >= 5) & (present > 0)
    patch_idx = jnp.maximum(local_row - 5, 0)
    coord_y = jnp.where(
        is_patch,
        (2.0 * (patch_idx // breadth).astype(jnp.float32) + 1.0) / height.astype(jnp.float32) - 1.0,
        0.0,
    )
    coord_x = jnp.where(
        is_patch,
        (2.0 * (patch_idx % breadth).astype(jnp.float32) + 1.0) / breadth.astype(jnp.float32) - 1.0,
        0.0,
    )
    quarter = head_size // 4
    frequency = math.pi * 100.0 ** (-jnp.arange(quarter, dtype=jnp.float32) / quarter)
    angle_y = (coord_y[:, None] * frequency[None, :])[:, None, :]
    angle_x = (coord_x[:, None] * frequency[None, :])[:, None, :]
    return (image_id, (jnp.cos(angle_y), jnp.sin(angle_y), jnp.cos(angle_x), jnp.sin(angle_x)))


def rotate(vectors, tables):
    cos_y, sin_y, cos_x, sin_x = tables
    quarter = vectors.shape[-1] // 4
    upper_y = vectors[..., :quarter]
    lower_y = vectors[..., quarter : 2 * quarter]
    upper_x = vectors[..., 2 * quarter : 3 * quarter]
    lower_x = vectors[..., 3 * quarter :]
    return jnp.concatenate(
        [
            upper_y * cos_y - lower_y * sin_y,
            upper_y * sin_y + lower_y * cos_y,
            upper_x * cos_x - lower_x * sin_x,
            upper_x * sin_x + lower_x * cos_x,
        ],
        axis=-1,
    )


def attend(queries, key_rows, values, image_id, numbers):
    scores = jnp.einsum(
        "qhd,khd->hqk", queries, key_rows, preferred_element_type=jnp.float32
    ) / math.sqrt(queries.shape[-1])
    same_image = image_id[:, None] == image_id[None, :]
    scores = jnp.where(same_image[None], scores, -jnp.inf)
    row_peak = jnp.max(scores, axis=-1)
    expo_vals = jnp.exp(scores - row_peak[..., None])
    weights = (expo_vals / jnp.sum(expo_vals, axis=-1, keepdims=True)).astype(jnp.bfloat16)
    attended = jnp.einsum(
        "hqk,khd->qhd", weights, values, preferred_element_type=jnp.float32
    ).astype(jnp.bfloat16)
    owned = image_id[None, None, :] == numbers[:, None, None]
    logits = jnp.max(jnp.where(owned, row_peak[None], -jnp.inf), axis=-1)
    return (attended, logits)


def on_device(
    tokens,
    grid_sides,
    offsets,
    merge_rows,
    routes,
    norm_gain,
    norm_bias,
    layer_scale,
    qkv_weight,
    out_weight,
    gate_up,
    down_weight,
    merge_gain,
    merge_bias,
    merge_weight,
):
    row_count = tokens.shape[0]
    model_width = tokens.shape[1]
    groups = lax.axis_size("req")
    shards = lax.axis_size("mlp")
    group_id = lax.axis_index("req")
    member = lax.axis_index("mlp")
    piece_width = model_width // shards
    start_col = member * piece_width
    slot_count = merge_rows.shape[0]
    numbers = jnp.arange(grid_sides.shape[0], dtype=jnp.int32)
    image_id, tables = row_layout(grid_sides, offsets, row_count, HEAD)
    normed = layer_norm(tokens.astype(jnp.float32), norm_gain[0], norm_bias[0]).astype(jnp.bfloat16)
    columns = normed
    mixed_qkv = jnp.dot(
        columns,
        lax.all_gather(qkv_weight, "req", axis=0, tiled=True),
        preferred_element_type=jnp.float32,
    )
    heads_here = qkv_weight.shape[1] // (3 * HEAD)
    mixed_qkv = mixed_qkv.reshape(row_count, heads_here, 3, HEAD)
    queries = rotate(mixed_qkv[:, :, 0], tables).astype(jnp.bfloat16)
    key_rows = rotate(mixed_qkv[:, :, 1], tables).astype(jnp.bfloat16)
    values = mixed_qkv[:, :, 2].astype(jnp.bfloat16)
    attended, logits = attend(queries, key_rows, values, image_id, numbers)
    attended_flat = attended.reshape(row_count, heads_here * HEAD)
    head_terms = jnp.dot(
        attended_flat,
        lax.all_gather(out_weight, "req", axis=1, tiled=True),
        preferred_element_type=jnp.float32,
    )
    attn_sum = lax.psum(head_terms.astype(jnp.bfloat16), "mlp").astype(jnp.float32)
    residual = (tokens.astype(jnp.float32) + layer_scale[0] * attn_sum).astype(jnp.bfloat16)
    resid_piece = lax.dynamic_slice_in_dim(residual, start_col, piece_width, 1)
    normed_two = layer_norm(residual.astype(jnp.float32), norm_gain[1], norm_bias[1]).astype(
        jnp.bfloat16
    )
    columns = normed_two
    gate_pair = jnp.einsum(
        "rk,pkn->prn",
        columns,
        lax.all_gather(gate_up, "req", axis=1, tiled=True),
        preferred_element_type=jnp.float32,
    )
    hidden = (jax.nn.silu(gate_pair[0]) * gate_pair[1]).astype(jnp.bfloat16)
    hidden_terms = jnp.dot(
        hidden,
        lax.all_gather(down_weight, "req", axis=1, tiled=True),
        preferred_element_type=jnp.float32,
    )
    ffn_piece = lax.psum_scatter(
        hidden_terms.astype(jnp.bfloat16), "mlp", scatter_dimension=1, tiled=True
    ).astype(jnp.float32)
    own_scale_two = lax.dynamic_slice_in_dim(layer_scale[1], start_col, piece_width, 0)
    final_piece = (resid_piece.astype(jnp.float32) + own_scale_two * ffn_piece).astype(jnp.bfloat16)
    merged = final_piece[merge_rows].astype(jnp.float32)
    totals, squares = lax.psum(
        (jnp.sum(merged, axis=(1, 2)), jnp.sum(merged * merged, axis=(1, 2))), "mlp"
    )
    center = totals / (4 * model_width)
    spread = squares / (4 * model_width) - center * center
    scaled = (
        (merged - center[:, None, None]) * lax.rsqrt(spread + EPS)[:, None, None] * merge_gain[None]
        + merge_bias[None]
    ).astype(jnp.bfloat16)
    scaled_flat = scaled.reshape(slot_count, 4 * piece_width)
    piece_rows = lax.all_gather(merge_weight, "req", axis=2, tiled=True)
    merge_terms = jnp.dot(
        scaled_flat,
        piece_rows.reshape(4 * piece_width, piece_rows.shape[2]),
        preferred_element_type=jnp.float32,
    )
    projected = lax.psum_scatter(
        merge_terms.astype(jnp.bfloat16), "mlp", scatter_dimension=1, tiled=True
    ).astype(jnp.float32)
    slot_ids = jnp.arange(slot_count, dtype=jnp.int32)
    owner_grid = grid_sides[slot_ids // MSLOT]
    is_live = slot_ids % MSLOT < owner_grid[:, 0] // 2 * (owner_grid[:, 1] // 2)
    projected = jnp.where(is_live[:, None], projected, 0.0).astype(jnp.bfloat16)
    out_cols = projected.shape[1]
    own_routes = lax.dynamic_slice_in_dim(routes, group_id * slot_count, slot_count, 0)[:, 0]
    onehot = (own_routes[:, None] == jnp.arange(groups, dtype=jnp.int32)[None, :]).astype(jnp.int32)
    before = jnp.cumsum(onehot, axis=0) - onehot
    ranks = jnp.sum(before * onehot, axis=1)
    send_rows = (
        jnp.zeros((groups * CAP, out_cols), jnp.bfloat16)
        .at[own_routes * CAP + ranks]
        .set(projected)
    )
    received = lax.all_to_all(
        send_rows.reshape(groups, CAP, out_cols), "req", split_axis=0, concat_axis=0, tiled=True
    )
    embeds = received.reshape(groups * CAP, out_cols)
    row_squares = jnp.sum(jnp.square(embeds.astype(jnp.float32)), axis=1)
    total_squares = lax.psum(row_squares, "mlp")
    token_norms = jnp.sqrt(total_squares / OUT + EPS)
    return (embeds, token_norms, logits)


def solution(mesh):
    placed = (
        P("req", None),
        P("req", None),
        P("req"),
        P("req", None),
        P(),
        P(),
        P(),
        P(),
        P("req", "mlp"),
        P("mlp", "req"),
        P(None, "req", "mlp"),
        P("mlp", "req"),
        P(None, "mlp"),
        P(None, "mlp"),
        P(None, "mlp", "req"),
    )
    return jax.shard_map(
        on_device,
        mesh=mesh,
        in_specs=placed,
        out_specs=(P("req", "mlp"), P("req"), P("req", "mlp")),
        check_vma=False,
    )
```

profile of v0, /device:TPU:0, one launch (start us, length us, event | category | flops | bytes accessed | tf_op | source)
XLA Modules:
  0.0 1053.9 jit_solution(7051907031724275753)
XLA Ops:
  7.2 0.7 all-gather.6.cloned.1.call-update
  8.0 0.7 all-gather.8.cloned.1.call-update
  8.7 1.1 slice_reduce_fusion
  9.8 0.9 add_add_fusion.1
  10.7 0.8 select_reduce_fusion.5
  11.5 2.8 convert_reduce_fusion
  14.3 1.2 fusion.4
  15.9 3.0 multiply_cosine_fusion.1
  19.0 170.4 %all-gather.6.cloned.1.call-done = bf16[4096,1536]{1,0:T(8,128)(2,1)} async-done(((bf16[512,1536]{1,0:T(8,128)(2,1)}), bf16[4096,1536]{1,0:T(8,128)(2,1)}) %all-gather.6.cloned.1.call-update) | async-done | bytes 12582928 | tf_op jit(solution)/shard_map/all_gather | solution.py:119
  189.4 11.7 %fusion.16 = f32[512,1536]{0,1:T(8,128)S(1)} fusion(bf16[4096,1536]{1,0:T(8,128)(2,1)} %all-gather.6.cloned.1.call-done, bf16[512,4096]{1,0:T(8,128)(2,1)} %param.15, f32[4096]{0:T(1024)S(1)} %bitcast.60, f32[4096]{0:T(1024)S(1)} %bitcast.59, f32[512]{0:T(512)S(1)} %add_rsqrt_fusion.1, f32[512]{0:T(512)S(1)} %broadcast_multiply_fusion.1), kind=kOutput, calls=%fused_computation.25 | convolution fusion | flops 6455033856 | bytes 19959808 | tf_op jit(solution)/shard_map/dot_general | solution.py:117
  201.2 1.5 copy-done.8
  202.7 0.3 copy.46
  203.0 0.3 copy.47
  203.4 2.2 subtract_convert_fusion.3
  205.6 0.9 subtract_convert_fusion.1
  206.5 2.1 fusion.26
  208.6 0.9 fusion.27
  209.5 2.7 fusion.39
  212.2 52.4 %all-gather.8.cloned.1.call-done = bf16[512,4096]{1,0:T(8,128)(2,1)} async-done(((bf16[512,512]{1,0:T(8,128)(2,1)}), bf16[512,4096]{1,0:T(8,128)(2,1)}) %all-gather.8.cloned.1.call-update) | async-done | bytes 4194320 | tf_op jit(solution)/shard_map/all_gather | solution.py:131
  264.6 6.5 convolution_convert_fusion.1
  271.2 0.5 all-gather.10.cloned.1.call-update
  271.8 0.5 all-gather.12.cloned.1.call-update
  272.7 82.3 %all-reduce.3.cloned.1.call-done = bf16[512,4096]{1,0:T(8,128)(2,1)} async-done(((bf16[512,4096]{1,0:T(8,128)(2,1)}), bf16[512,4096]{1,0:T(8,128)(2,1)}) %all-reduce.3.cloned.1.call-update) | async-done | bytes 4194320 | tf_op jit(solution)/shard_map/psum | solution.py:134
  355.0 5.6 convert_reduce_fusion.1
  360.6 1.9 copy-done.3
  362.5 1.2 fusion.8
  363.7 221.3 %all-gather.10.cloned.1.call-done = bf16[2,4096,1024]{2,1,0:T(8,128)(2,1)} async-done(((bf16[2,512,1024]{2,1,0:T(8,128)(2,1)}), bf16[2,4096,1024]{2,1,0:T(8,128)(2,1)}) %all-gather.10.cloned.1.call-update) | async-done | bytes 16777232 | tf_op jit(solution)/shard_map/all_gather | solution.py:144
  585.1 15.0 %fusion.29 = f32[2,512,1024]{2,1,0:T(8,128)} fusion(bf16[2,4096,1024]{2,1,0:T(8,128)(2,1)} %all-gather.10.cloned.1.call-done, bf16[512,4096]{1,0:T(8,128)(2,1)} %copy-done.3, f32[4096]{0:T(1024)S(1)} %bitcast.58, f32[4096]{0:T(1024)S(1)} %bitcast.57, f32[512]{0:T(512)S(1)} %add_rsqrt_fusion, f32[512]{0:T(512)S(1)} %broadcast_multiply_fusion), kind=kOutput, calls=%fused_computation.41 | convolution fusion | flops 8602517504 | bytes 25202688 | tf_op jit(solution)/shard_map/rk,pkn->prn/dot_general | solution.py:141
  600.1 110.7 %all-gather.12.cloned.1.call-done = bf16[1024,4096]{1,0:T(8,128)(2,1)} async-done(((bf16[1024,512]{1,0:T(8,128)(2,1)}), bf16[1024,4096]{1,0:T(8,128)(2,1)}) %all-gather.12.cloned.1.call-update) | async-done | bytes 8388624 | tf_op jit(solution)/shard_map/all_gather | solution.py:150
  710.8 11.2 %convolution_convert_fusion = bf16[512,4096]{1,0:T(8,128)(2,1)} fusion(bf16[1024,4096]{1,0:T(8,128)(2,1)} %all-gather.12.cloned.1.call-done, f32[2,512,1024]{2,1,0:T(8,128)} %fusion.29), kind=kOutput, calls=%fused_computation.21 | convolution fusion | flops 4300210176 | bytes 16777216 | tf_op jit(solution)/shard_map/dot_general | solution.py:148
  722.0 0.7 all-gather.14.cloned.1.call-update
  723.3 41.5 %reduce-scatter.3.cloned.1.call-done = bf16[512,1024]{1,0:T(8,128)(2,1)} async-done(((bf16[512,4096]{1,0:T(8,128)(2,1)}), bf16[512,1024]{1,0:T(8,128)(2,1)}) %reduce-scatter.3.cloned.1.call-update) | async-done | bytes 1048592 | tf_op jit(solution)/shard_map/reduce_scatter | solution.py:153
  764.8 2.0 add_convert_fusion
  766.8 2.1 gather_fusion.1
  768.8 0.7 reshape.383
  770.0 1.0 multiply_reduce_fusion
  771.0 5.7 all-reduce
  776.8 217.8 %all-gather.14.cloned.1.call-done = bf16[4,1024,2048]{2,1,0:T(8,128)(2,1)} async-done(((bf16[4,1024,256]{2,1,0:T(8,128)(2,1)}), bf16[4,1024,2048]{2,1,0:T(8,128)(2,1)}) %all-gather.14.cloned.1.call-update) | async-done | bytes 16777232 | tf_op jit(solution)/shard_map/all_gather | solution.py:169
  994.6 10.1 fusion.28
  1005.7 0.6 gather_fusion
  1006.6 18.2 %reduce-scatter.5.cloned.1.call-done = bf16[128,512]{1,0:T(8,128)(2,1)} async-done(((bf16[128,2048]{1,0:T(8,128)(2,1)}), bf16[128,512]{1,0:T(8,128)(2,1)}) %reduce-scatter.5.cloned.1.call-update) | async-done | bytes 131088 | tf_op jit(solution)/shard_map/reduce_scatter | solution.py:175
  1024.8 2.1 scatter_custom_fusion
  1026.9 5.5 all-to-all-start
  1032.4 0.7 select_reduce_fusion.1
  1033.1 6.7 all-to-all-done
  1040.0 5.9 psum.31
  1045.9 0.5 add_sqrt_fusion
  1046.4 0.7 copy.66
  (74 shorter events, 3.5 us)
Async XLA Ops:
  7.2 997.6 %copy-start = (s32[1024,1]{0,1:T(1,128)S(1)}, s32[1024,1]{0,1:T(1,128)}, u32[]{:S(2)}) copy-start(s32[1024,1]{0,1:T(1,128)} %param.19) | copy-start | bytes 12292
  7.2 182.2 %all-gather.6.cloned.1.call-start = ((), (), s32[]{:S(2)}) async-start(), calls=%async_computation.3 | async-start | bytes 14155776 | tf_op jit(solution)/shard_map/all_gather | solution.py:119
  7.9 256.7 %all-gather.8.cloned.1.call-start = ((), (), s32[]{:S(2)}) async-start(), calls=%async_computation.4 | async-start | bytes 4718592 | tf_op jit(solution)/shard_map/all_gather | solution.py:131
  8.7 346.4 %all-reduce.3.cloned.1.call-start = ((), (), s32[]{:S(2)}) async-start(), calls=%async_computation.5 | async-start | bytes 8388608 | tf_op jit(solution)/shard_map/psum | solution.py:134
  8.7 5.6 copy-start.2
  11.4 7.5 copy-start.11
  11.4 7.5 copy-start.12
  201.0 1.7 copy-start.8
  203.4 2.2 copy-start.4
  203.4 2.2 copy-start.5
  203.4 2.2 copy-start.6
  203.4 2.2 copy-start.7
  271.2 1.5 copy-start.13
  271.2 313.9 %all-gather.10.cloned.1.call-start = ((), (), s32[]{:S(2)}) async-start(), calls=%async_computation.6 | async-start | bytes 18874368 | tf_op jit(solution)/shard_map/all_gather | solution.py:144
  271.8 439.0 %all-gather.12.cloned.1.call-start = ((), (), s32[]{:S(2)}) async-start(), calls=%async_computation.7 | async-start | bytes 9437184 | tf_op jit(solution)/shard_map/all_gather | solution.py:150
  272.4 492.4 %reduce-scatter.3.cloned.1.call-start = ((), (), s32[]{:S(2)}) async-start(), calls=%async_computation.8 | async-start | bytes 5242880 | tf_op jit(solution)/shard_map/reduce_scatter | solution.py:153
  360.6 1.9 copy-start.3
  721.9 1.1 copy-start.14
  721.9 272.7 %all-gather.14.cloned.1.call-start = ((), (), s32[]{:S(2)}) async-start(), calls=%async_computation.9 | async-start | bytes 18874368 | tf_op jit(solution)/shard_map/all_gather | solution.py:169
  722.7 302.1 %reduce-scatter.5.cloned.1.call-start = ((), (), s32[]{:S(2)}) async-start(), calls=%async_computation.10 | async-start | bytes 655360 | tf_op jit(solution)/shard_map/reduce_scatter | solution.py:175
  768.8 225.8 %copy-start.9 = (f32[4,1024]{1,0:T(4,128)S(1)}, f32[4,1024]{1,0:T(4,128)}, u32[]{:S(2)}) copy-start(f32[4,1024]{1,0:T(4,128)} %param.28) | copy-start | bytes 49156
  768.8 225.8 %copy-start.10 = (f32[4,1024]{1,0:T(4,128)S(1)}, f32[4,1024]{1,0:T(4,128)}, u32[]{:S(2)}) copy-start(f32[4,1024]{1,0:T(4,128)} %param.27) | copy-start | bytes 49156
  994.6 11.0 %copy-start.1 = (s32[2,2]{1,0:T(2,128)S(1)}, s32[2,2]{1,0:T(2,128)}, u32[]{:S(2)}) copy-start(s32[2,2]{1,0:T(2,128)} %param.16) | copy-start | bytes 52
  1026.9 12.9 %all-to-all-start = ((bf16[8,16,512]{2,1,0:T(8,128)(2,1)}), bf16[8,16,512]{2,1,0:T(8,128)(2,1)S(1)}, u32[]{:S(2)}, u32[]{:S(2)}) async-start(bf16[8,16,512]{2,1,0:T(8,128)(2,1)} %bitcast.18), calls=%async_computation.2 | async-start | bytes 262144 | tf_op jit(solution)/shard_map/all_to_all | solution.py:192
Sparse Core Ops, SparseCore 0:
  10.2 179.1 all-gather.5
  191.4 73.1 all-gather.7
  271.3 83.6 all-reduce.2
  357.3 227.7 all-gather.9
  587.1 123.5 all-gather.11
  722.1 42.6 reduce-scatter.2
  766.8 227.7 all-gather.13
  1004.9 19.8 reduce-scatter.4
where the time goes:
time: 1050 us
  waiting for transfers between devices  925 us (88%)
  matrix products  59.2 us (6%)
  other arithmetic  27.4 us (3%)
  between operations  14.5 us (1%)
  blocking collectives  11.6 us (1%)
    all_gather x1, waiting for transfers between devices, on_device(): lax.all_gather(gate_up, 'req', axis=1, tiled=True)  221 us
    all_gather x1, waiting for transfers between devices, on_device(): piece_rows = lax.all_gather(merge_weight, 'req', axis=2, tiled=True)  218 us
    all_gather x1, waiting for transfers between devices, on_device(): lax.all_gather(qkv_weight, 'req', axis=0, tiled=True)  170 us
    all_gather x1, waiting for transfers between devices, on_device(): lax.all_gather(down_weight, 'req', axis=1, tiled=True)  111 us
    psum x1, waiting for transfers between devices, on_device(): lax.psum(head_terms.astype(jnp.bfloat16), 'mlp').astype(jnp.float32)  82.3 us
    all_gather x1, waiting for transfers between devices, on_device(): lax.all_gather(out_weight, 'req', axis=1, tiled=True)  52.4 us
    reduce_scatter x1, waiting for transfers between devices, on_device(): lax.psum_scatter(hidden_terms.astype(jnp.bfloat16), 'mlp', scatter_dimens...  41.5 us
  transfers between devices with their start and end apart: 9, of which 9 were waited for; matrix products, arithmetic and copies ran while one was open for 6% of the time, Pallas kernels for 0%

commit v1 on v0

--- a/solution.py
+++ b/solution.py
@@ -3,6 +3,7 @@
 import jax.numpy as jnp
 from jax import lax
 from jax.sharding import PartitionSpec as P
+from jax.lax import axis_index, axis_size, ppermute
 
 HEAD = 128
 OUT = 2048
@@ -138,12 +139,26 @@
         jnp.bfloat16
     )
     columns = normed_two
+    view_out, y_new = (axis_size("req"), axis_index("req"))
+    chunks = tuple(((m, (m - 1) % view_out) for m in range(view_out)))
+    outcome_arr = gate_up.shape[1]
+    state_now = gate_up
     gate_pair = jnp.einsum(
         "rk,pkn->prn",
-        columns,
-        lax.all_gather(gate_up, "req", axis=1, tiled=True),
-        preferred_element_type=jnp.float32,
-    )
+        lax.dynamic_slice_in_dim(columns, y_new * outcome_arr, state_now.shape[1], axis=1),
+        state_now,
+        preferred_element_type=jnp.float32,
+    )
+    for j0 in [*range(1, view_out)]:
+        state_now = ppermute(state_now, "req", perm=chunks)
+        gate_pair = gate_pair + jnp.einsum(
+            "rk,pkn->prn",
+            lax.dynamic_slice_in_dim(
+                columns, (y_new + j0) % view_out * outcome_arr, state_now.shape[1], axis=1
+            ),
+            state_now,
+            preferred_element_type=jnp.float32,
+        )
     hidden = (jax.nn.silu(gate_pair[0]) * gate_pair[1]).astype(jnp.bfloat16)
     hidden_terms = jnp.dot(
         hidden,

time: 1050 us -> 1040 us (level)
  waiting for transfers between devices: 925 us -> 857 us
  starting transfers between devices: 6.32 us -> 38.9 us
  matrix products: 59.2 us -> 74.9 us
    ppermute x0 -> x7, waiting for transfers between devices: none -> 354 us  [on_device(): state_now = ppermute(state_now, 'req', perm=chunks)]
    all_gather x1 -> x0, waiting for transfers between devices: 221 us -> none  [on_device(): lax.all_gather(gate_up, 'req', axis=1, tiled=True)]
    all_gather x1, waiting for transfers between devices: 111 us -> 0.01 us  [on_device(): lax.all_gather(down_weight, 'req', axis=1, tiled=True)]
    psum x1, waiting for transfers between devices: 82.3 us -> 0.01 us  [on_device(): lax.psum(head_terms.astype(jnp.bfloat16), 'mlp').astype(jnp.float32)]
    ppermute x0 -> x7, starting transfers between devices: none -> 32.9 us  [on_device(): state_now = ppermute(state_now, 'req', perm=chunks)]
    dot_general x1 -> x8, matrix products: 15 us -> 30.4 us  [the longest x7 29.2 us: on_device(): jnp.einsum('rk,pkn->prn', lax.dynamic_slice_in_dim(columns, (y_new + j0)...]
    all_gather x1, waiting for transfers between devices: 170 us -> 158 us  [on_device(): lax.all_gather(qkv_weight, 'req', axis=0, tiled=True)]
  transfers between devices with their start and end apart: 9 -> 15, of which waited for: 9 -> 12; matrix products, arithmetic and copies ran while one was open for 6% -> 8% of each run, Pallas kernels for 0% -> 0%
where the time goes in v1:
time: 1040 us
  waiting for transfers between devices  857 us (82%)
  matrix products  74.9 us (7%)
  starting transfers between devices  38.9 us (4%)
  other arithmetic  28.6 us (3%)
  between operations  14.9 us (1%)
  blocking collectives  11.7 us (1%)
  local copies, waits for them, and re-layouts  11.4 us (1%)
    ppermute x7, waiting for transfers between devices, on_device(): state_now = ppermute(state_now, 'req', perm=chunks)  354 us
    all_gather x1, waiting for transfers between devices, on_device(): piece_rows = lax.all_gather(merge_weight, 'req', axis=2, tiled=True)  218 us
    all_gather x1, waiting for transfers between devices, on_device(): lax.all_gather(qkv_weight, 'req', axis=0, tiled=True)  158 us
    all_gather x1, waiting for transfers between devices, on_device(): lax.all_gather(out_weight, 'req', axis=1, tiled=True)  55.5 us
    reduce_scatter x1, waiting for transfers between devices, on_device(): lax.psum_scatter(hidden_terms.astype(jnp.bfloat16), 'mlp', scatter_dimens...  45.6 us
    ppermute x7, starting transfers between devices, on_device(): state_now = ppermute(state_now, 'req', perm=chunks)  32.9 us
    dot_general x7, matrix products, on_device(): jnp.einsum('rk,pkn->prn', lax.dynamic_slice_in_dim(columns, (y_new + j0)...  29.2 us
  transfers between devices with their start and end apart: 15, of which 12 were waited for; matrix products, arithmetic and copies ran while one was open for 8% of the time, Pallas kernels for 0%

profile of v1, /device:TPU:0, one launch (start us, length us, event | category | flops | bytes accessed | tf_op | source)
XLA Modules:
  0.0 1037.5 jit_solution(666846459537921218)
XLA Ops:
  8.0 6.0 collective-permute-start
  15.2 3.0 convert_reduce_fusion
  18.2 1.2 fusion.4
  20.0 3.0 multiply_cosine_fusion.1
  23.1 73.2 %collective-permute-done = bf16[2,512,1024]{2,1,0:T(8,128)(2,1)} collective-permute-done((bf16[2,512,1024]{2,1,0:T(8,128)(2,1)}, bf16[2,512,1024]{2,1,0:T(8,128)(2,1)}, u32[]{:S(2)}, u32[]{:S(2)}) %collective-permute-start) | collective-permute-done | bytes 2097184 | tf_op jit(solution)/shard_map/ppermute | solution.py:153
  96.3 5.2 collective-permute-start.1
  101.5 157.9 %all-gather.5.cloned.1.call-done = bf16[4096,1536]{1,0:T(8,128)(2,1)} async-done(((bf16[512,1536]{1,0:T(8,128)(2,1)}), bf16[4096,1536]{1,0:T(8,128)(2,1)}) %all-gather.5.cloned.1.call-update) | async-done | bytes 12582928 | tf_op jit(solution)/shard_map/all_gather | solution.py:120
  259.4 11.8 %fusion.13 = f32[512,1536]{0,1:T(8,128)S(1)} fusion(bf16[4096,1536]{1,0:T(8,128)(2,1)} %all-gather.5.cloned.1.call-done, bf16[512,4096]{1,0:T(8,128)(2,1)} %param.15, f32[4096]{0:T(1024)S(1)} %bitcast.86, f32[4096]{0:T(1024)S(1)} %bitcast.85, f32[512]{0:T(512)S(1)} %add_rsqrt_fusion.1, f32[512]{0:T(512)S(1)} %broadcast_multiply_fusion.1), kind=kOutput, calls=%fused_computation.23 | convolution fusion | flops 6455033856 | bytes 19959808 | tf_op jit(solution)/shard_map/dot_general | solution.py:118
  271.4 1.5 copy-done.12
  273.6 2.2 subtract_convert_fusion.1
  276.7 2.1 fusion.19
  279.7 2.7 fusion.29
  282.4 55.5 %all-gather.7.cloned.1.call-done = bf16[512,4096]{1,0:T(8,128)(2,1)} async-done(((bf16[512,512]{1,0:T(8,128)(2,1)}), bf16[512,4096]{1,0:T(8,128)(2,1)}) %all-gather.7.cloned.1.call-update) | async-done | bytes 4194320 | tf_op jit(solution)/shard_map/all_gather | solution.py:132
  337.9 6.6 convolution_convert_fusion.1
  344.5 1.5 collective-permute-start.2
  346.1 46.0 %collective-permute-done.2 = bf16[2,512,1024]{2,1,0:T(8,128)(2,1)S(1)} collective-permute-done((bf16[2,512,1024]{2,1,0:T(8,128)(2,1)}, bf16[2,512,1024]{2,1,0:T(8,128)(2,1)S(1)}, u32[]{:S(2)}, u32[]{:S(2)}) %collective-permute-start.2) | collective-permute-done | bytes 2097184 | tf_op jit(solution)/shard_map/ppermute | solution.py:153
  392.1 4.3 collective-permute-start.3
  396.4 45.3 %collective-permute-done.3 = bf16[2,512,1024]{2,1,0:T(8,128)(2,1)S(1)} collective-permute-done((bf16[2,512,1024]{2,1,0:T(8,128)(2,1)S(1)}, bf16[2,512,1024]{2,1,0:T(8,128)(2,1)S(1)}, u32[]{:S(2)}, u32[]{:S(2)}) %collective-permute-start.3) | collective-permute-done | bytes 2097184 | tf_op jit(solution)/shard_map/ppermute | solution.py:153
  441.8 1.3 copy-done.10
  443.1 5.3 collective-permute-start.4
  448.4 71.0 %collective-permute-done.4 = bf16[2,512,1024]{2,1,0:T(8,128)(2,1)} collective-permute-done((bf16[2,512,1024]{2,1,0:T(8,128)(2,1)S(1)}, bf16[2,512,1024]{2,1,0:T(8,128)(2,1)}, u32[]{:S(2)}, u32[]{:S(2)}) %collective-permute-start.4) | collective-permute-done | bytes 2097184 | tf_op jit(solution)/shard_map/ppermute | solution.py:153
  519.3 5.3 collective-permute-start.5
  524.7 88.6 %collective-permute-done.5 = bf16[2,512,1024]{2,1,0:T(8,128)(2,1)} collective-permute-done((bf16[2,512,1024]{2,1,0:T(8,128)(2,1)}, bf16[2,512,1024]{2,1,0:T(8,128)(2,1)}, u32[]{:S(2)}, u32[]{:S(2)}) %collective-permute-start.5) | collective-permute-done | bytes 2097184 | tf_op jit(solution)/shard_map/ppermute | solution.py:153
  613.3 5.2 collective-permute-start.6
  618.5 5.6 convert_reduce_fusion.1
  625.4 2.4 fusion.11
  627.9 1.3 fusion.67
  629.1 1.8 copy-done.11
  630.9 1.3 fusion.59
  632.2 1.3 fusion.61
  633.5 2.9 fusion.63
  636.4 4.8 fusion.57
  641.2 4.8 fusion.65
  646.0 4.8 fusion.55
  650.8 30.3 %collective-permute-done.6 = bf16[2,512,1024]{2,1,0:T(8,128)(2,1)} collective-permute-done((bf16[2,512,1024]{2,1,0:T(8,128)(2,1)}, bf16[2,512,1024]{2,1,0:T(8,128)(2,1)}, u32[]{:S(2)}, u32[]{:S(2)}) %collective-permute-start.6) | collective-permute-done | bytes 2097184 | tf_op jit(solution)/shard_map/ppermute | solution.py:153
  681.2 9.3 add_bitcast_fusion
  690.5 11.2 %convolution_convert_fusion = bf16[512,4096]{1,0:T(8,128)(2,1)} fusion(bf16[1024,4096]{1,0:T(8,128)(2,1)} %all-gather.9.cloned.1.call-done, f32[2,512,1024]{2,1,0:T(8,128)} %add_bitcast_fusion), kind=kOutput, calls=%fused_computation.21 | convolution fusion | flops 4300210176 | bytes 16777216 | tf_op jit(solution)/shard_map/dot_general | solution.py:163
  702.8 45.6 %reduce-scatter.3.cloned.1.call-done = bf16[512,1024]{1,0:T(8,128)(2,1)} async-done(((bf16[512,4096]{1,0:T(8,128)(2,1)}), bf16[512,1024]{1,0:T(8,128)(2,1)}) %reduce-scatter.3.cloned.1.call-update) | async-done | bytes 1048592 | tf_op jit(solution)/shard_map/reduce_scatter | solution.py:168
  748.3 2.0 add_convert_fusion
  750.3 2.1 gather_fusion.1
  754.6 5.7 all-reduce
  760.3 217.7 %all-gather.11.cloned.1.call-done = bf16[4,1024,2048]{2,1,0:T(8,128)(2,1)} async-done(((bf16[4,1024,256]{2,1,0:T(8,128)(2,1)}), bf16[4,1024,2048]{2,1,0:T(8,128)(2,1)}) %all-gather.11.cloned.1.call-update) | async-done | bytes 16777232 | tf_op jit(solution)/shard_map/all_gather | solution.py:184
  978.0 10.1 fusion.21
  990.0 18.2 %reduce-scatter.5.cloned.1.call-done = bf16[128,512]{1,0:T(8,128)(2,1)} async-done(((bf16[128,2048]{1,0:T(8,128)(2,1)}), bf16[128,512]{1,0:T(8,128)(2,1)}) %reduce-scatter.5.cloned.1.call-update) | async-done | bytes 131088 | tf_op jit(solution)/shard_map/reduce_scatter | solution.py:190
  1008.2 2.1 scatter_custom_fusion
  1010.3 5.5 all-to-all-start
  1016.5 6.7 all-to-all-done
  1023.3 5.9 psum.31
  (103 shorter events, 13.6 us)
Async XLA Ops:
  7.2 981.0 %copy-start = (s32[1024,1]{0,1:T(1,128)S(1)}, s32[1024,1]{0,1:T(1,128)}, u32[]{:S(2)}) copy-start(s32[1024,1]{0,1:T(1,128)} %param.19) | copy-start | bytes 12292
  7.2 252.2 %all-gather.5.cloned.1.call-start = ((), (), s32[]{:S(2)}) async-start(), calls=%async_computation.3 | async-start | bytes 14155776 | tf_op jit(solution)/shard_map/all_gather | solution.py:120
  7.9 330.0 %all-gather.7.cloned.1.call-start = ((), (), s32[]{:S(2)}) async-start(), calls=%async_computation.4 | async-start | bytes 4718592 | tf_op jit(solution)/shard_map/all_gather | solution.py:132
  8.0 88.3 %collective-permute-start = (bf16[2,512,1024]{2,1,0:T(8,128)(2,1)}, bf16[2,512,1024]{2,1,0:T(8,128)(2,1)}, u32[]{:S(2)}, u32[]{:S(2)}) collective-permute-start(bf16[2,512,1024]{2,1,0:T(8,128)(2,1)} %param.25), channel_id=1, source_target_pairs={{0,28},{4,0},{8,4},{12,8},{16,12},{20,16},{24,20},{28,24},{1,29},{... | collective-permute-start | bytes 6291464 | tf_op jit(solution)/shard_map/ppermute | solution.py:153
  14.0 604.5 %all-reduce.3.cloned.1.call-start = ((), (), s32[]{:S(2)}) async-start(), calls=%async_computation.5 | async-start | bytes 8388608 | tf_op jit(solution)/shard_map/psum | solution.py:135
  14.1 4.2 copy-start.3
  15.1 4.3 copy-start.19
  15.1 7.9 copy-start.15
  15.2 7.9 copy-start.16
  96.3 248.2 %collective-permute-start.1 = (bf16[2,512,1024]{2,1,0:T(8,128)(2,1)}, bf16[2,512,1024]{2,1,0:T(8,128)(2,1)}, u32[]{:S(2)}, u32[]{:S(2)}) collective-permute-start(bf16[2,512,1024]{2,1,0:T(8,128)(2,1)} %collective-permute-done), channel_id=1, source_target_pairs={{0,28},{4,0},{8,4},{12,8},{16,12},{20,16},{24,20},{28,24},{1,29},{... | collective-permute-start | bytes 6291464 | tf_op jit(solution)/shard_map/ppermute | solution.py:153
  271.2 1.7 copy-start.12
  273.6 2.2 copy-start.5
  273.6 2.2 copy-start.6
  273.6 2.2 copy-start.7
  273.6 2.2 copy-start.8
  344.4 180.2 %copy-start.17 = (f32[2,4096]{1,0:T(2,128)S(1)}, f32[2,4096]{1,0:T(2,128)}, u32[]{:S(2)}) copy-start(f32[2,4096]{1,0:T(2,128)} %param.22) | copy-start | bytes 98308
  344.5 346.0 %all-gather.9.cloned.1.call-start = ((), (), s32[]{:S(2)}) async-start(), calls=%async_computation.6 | async-start | bytes 9437184 | tf_op jit(solution)/shard_map/all_gather | solution.py:165
  344.5 47.6 %collective-permute-start.2 = (bf16[2,512,1024]{2,1,0:T(8,128)(2,1)}, bf16[2,512,1024]{2,1,0:T(8,128)(2,1)S(1)}, u32[]{:S(2)}, u32[]{:S(2)}) collective-permute-start(bf16[2,512,1024]{2,1,0:T(8,128)(2,1)} %collective-permute-done.1), channel_id=1, source_target_pairs={{0,28},{4,0},{8,4},{12,8},{16,12},{20,16},{24,20},{28,24},{1,29},{... | collective-permute-start | bytes 6291464 | tf_op jit(solution)/shard_map/ppermute | solution.py:153
  346.0 402.3 %reduce-scatter.3.cloned.1.call-start = ((), (), s32[]{:S(2)}) async-start(), calls=%async_computation.7 | async-start | bytes 5242880 | tf_op jit(solution)/shard_map/reduce_scatter | solution.py:168
  392.1 49.7 %collective-permute-start.3 = (bf16[2,512,1024]{2,1,0:T(8,128)(2,1)S(1)}, bf16[2,512,1024]{2,1,0:T(8,128)(2,1)S(1)}, u32[]{:S(2)}, u32[]{:S(2)}) collective-permute-start(bf16[2,512,1024]{2,1,0:T(8,128)(2,1)S(1)} %collective-permute-done.2), channel_id=1, source_target_pairs={{0,28},{4,0},{8,4},{12,8},{16,12},{20,16},{24,20},{28,24},{1,29},{... | collective-permute-start | bytes 6291464 | tf_op jit(solution)/shard_map/ppermute | solution.py:153
  441.8 1.3 copy-start.10
  443.1 76.2 %collective-permute-start.4 = (bf16[2,512,1024]{2,1,0:T(8,128)(2,1)S(1)}, bf16[2,512,1024]{2,1,0:T(8,128)(2,1)}, u32[]{:S(2)}, u32[]{:S(2)}) collective-permute-start(bf16[2,512,1024]{2,1,0:T(8,128)(2,1)S(1)} %collective-permute-done.3), channel_id=1, source_target_pairs={{0,28},{4,0},{8,4},{12,8},{16,12},{20,16},{24,20},{28,24},{1,29},{... | collective-permute-start | bytes 6291464 | tf_op jit(solution)/shard_map/ppermute | solution.py:153
  519.3 94.0 %collective-permute-start.5 = (bf16[2,512,1024]{2,1,0:T(8,128)(2,1)}, bf16[2,512,1024]{2,1,0:T(8,128)(2,1)}, u32[]{:S(2)}, u32[]{:S(2)}) collective-permute-start(bf16[2,512,1024]{2,1,0:T(8,128)(2,1)} %collective-permute-done.4), channel_id=1, source_target_pairs={{0,28},{4,0},{8,4},{12,8},{16,12},{20,16},{24,20},{28,24},{1,29},{... | collective-permute-start | bytes 6291464 | tf_op jit(solution)/shard_map/ppermute | solution.py:153
  613.3 67.9 %collective-permute-start.6 = (bf16[2,512,1024]{2,1,0:T(8,128)(2,1)}, bf16[2,512,1024]{2,1,0:T(8,128)(2,1)}, u32[]{:S(2)}, u32[]{:S(2)}) collective-permute-start(bf16[2,512,1024]{2,1,0:T(8,128)(2,1)} %collective-permute-done.5), channel_id=1, source_target_pairs={{0,28},{4,0},{8,4},{12,8},{16,12},{20,16},{24,20},{28,24},{1,29},{... | collective-permute-start | bytes 6291464 | tf_op jit(solution)/shard_map/ppermute | solution.py:153
  624.1 3.7 copy-start.2
  625.4 2.5 copy-start.9
  627.8 18.2 %copy-start.4 = (bf16[512,4096]{1,0:T(8,128)(2,1)}, bf16[512,4096]{1,0:T(8,128)(2,1)S(1)}, u32[]{:S(2)}) copy-start(bf16[512,4096]{1,0:T(8,128)(2,1)S(1)} %fusion.11) | copy-start | bytes 12582916
  627.8 3.1 copy-start.11
  701.6 0.9 copy-start.18
  701.7 276.4 %all-gather.11.cloned.1.call-start = ((), (), s32[]{:S(2)}) async-start(), calls=%async_computation.8 | async-start | bytes 18874368 | tf_op jit(solution)/shard_map/all_gather | solution.py:184
  702.2 306.0 %reduce-scatter.5.cloned.1.call-start = ((), (), s32[]{:S(2)}) async-start(), calls=%async_computation.9 | async-start | bytes 655360 | tf_op jit(solution)/shard_map/reduce_scatter | solution.py:190
  752.4 225.7 %copy-start.13 = (f32[4,1024]{1,0:T(4,128)S(1)}, f32[4,1024]{1,0:T(4,128)}, u32[]{:S(2)}) copy-start(f32[4,1024]{1,0:T(4,128)} %param.28) | copy-start | bytes 49156
  752.4 225.7 %copy-start.14 = (f32[4,1024]{1,0:T(4,128)S(1)}, f32[4,1024]{1,0:T(4,128)}, u32[]{:S(2)}) copy-start(f32[4,1024]{1,0:T(4,128)} %param.27) | copy-start | bytes 49156
  978.0 11.0 %copy-start.1 = (s32[2,2]{1,0:T(2,128)S(1)}, s32[2,2]{1,0:T(2,128)}, u32[]{:S(2)}) copy-start(s32[2,2]{1,0:T(2,128)} %param.16) | copy-start | bytes 52
  1010.3 12.8 %all-to-all-start = ((bf16[8,16,512]{2,1,0:T(8,128)(2,1)}), bf16[8,16,512]{2,1,0:T(8,128)(2,1)S(1)}, u32[]{:S(2)}, u32[]{:S(2)}) async-start(bf16[8,16,512]{2,1,0:T(8,128)(2,1)} %bitcast.25), calls=%async_computation.2 | async-start | bytes 262144 | tf_op jit(solution)/shard_map/all_to_all | solution.py:207
Sparse Core Ops, SparseCore 0:
  10.2 249.1 all-gather.4
  261.4 76.4 all-gather.6
  344.6 83.6 all-reduce.2
  430.4 227.3 all-gather.8
  701.8 46.5 reduce-scatter.2
  750.2 227.7 all-gather.10
  988.3 19.8 reduce-scatter.4
